TPU v7x, 32 devices: a whole 2x2x4 slice. The times are simulated.
32 devices in a mesh: kv: 4 (over y, x), ctx: 8 (over z, core).
Axes of the slice: x: 2, y: 2, z: 4, core: 2. Of those that a mesh axis runs over, the one named last changes fastest.
Arguments:
- queries: bfloat16 [1024, 8192], P('ctx', 'kv'), may hold values from -8 to 8
- key_cache: bfloat16 [32768, 1024], P('ctx', 'kv'), may hold values from -8 to 8
- value_cache: bfloat16 [32768, 1024], P('ctx', 'kv'), may hold values from -6 to 6
- blocks: int32 [8, 8, 32], replicated, may hold values from 0 to 255, as said below
- out_weight: bfloat16 [8192, 8192], P('kv', 'ctx'), may hold values from -0.0625 to 0.0625
Outputs:
- attended: bfloat16 [1024, 8192], P('kv', 'ctx')
Inputs may be any that keep to these rules, and one draw needn't show every extreme that they name: blocks[b, h, :] lists 32 distinct key blocks in ascending order, none after block 248 + b and always that block itself; each list names at most 7 of one cache device's 32 blocks, and a quarter of the 8 cache devices get 1, 3, 5 and 7 of its blocks each.
All inputs are finite; a program needn't handle non-finite values.
Results may differ from a plain program's by a relative error of at most 0.012.
Values may be sent and summed in bfloat16 or wider, within the bound.
A program may use at most 64 MiB of HBM per device.

v0:
```python
import math

import jax
import jax.numpy as jnp
from jax import lax
from jax.sharding import PartitionSpec as P

HD = 128
BLK = 128
MOST = 7


def shortened(x):
    return jax.tree.map(lambda a: a.astype(jnp.bfloat16) if a.dtype == jnp.float32 else a, x)


def shard_partials(
    queries_all, key_shard, value_shard, block_lists, shard_first, total_keys, head_count
):
    query_tokens = queries_all.shape[0]
    blocks_here = key_shard.shape[0] // BLK
    group_size = queries_all.shape[1] // (head_count * HD)
    score_scale = 1.0 / math.sqrt(HD)
    below = jnp.sum((block_lists < shard_first).astype(jnp.int32), axis=-1)
    inside = jnp.sum(
        ((block_lists >= shard_first) & (block_lists < shard_first + blocks_here)).astype(
            jnp.int32
        ),
        axis=-1,
    )
    slot_ids = jnp.arange(MOST, dtype=jnp.int32)
    places = jnp.clip(below[..., None] + slot_ids, 0, block_lists.shape[-1] - 1)
    picked = jnp.take_along_axis(block_lists, places, axis=-1) - shard_first
    usable = slot_ids < inside[..., None]
    picked = jnp.where(usable, picked, 0)
    key_blocks = key_shard.reshape(blocks_here, BLK, head_count, HD)
    value_blocks = value_shard.reshape(blocks_here, BLK, head_count, HD)
    offsets = jnp.arange(BLK, dtype=jnp.int32)

    def one_block(inputs):
        block_index, picked_now, usable_now = inputs
        rows_here = lax.dynamic_slice_in_dim(queries_all, block_index * BLK, BLK, 0)
        rows_here = rows_here.reshape(BLK, head_count, group_size, HD)
        query_pos = total_keys - query_tokens + block_index * BLK + offsets
        head_outputs, head_peaks, head_totals = ([], [], [])
        for head_index in range(head_count):
            chosen = picked_now[head_index]
            keys_taken = key_blocks[chosen, :, head_index, :].reshape(MOST * BLK, HD)
            values_taken = value_blocks[chosen, :, head_index, :].reshape(MOST * BLK, HD)
            key_pos = ((shard_first + chosen)[:, None] * BLK + offsets[None, :]).reshape(MOST * BLK)
            live_keys = jnp.repeat(usable_now[head_index], BLK)
            allowed = live_keys[None, :] & (key_pos[None, :] <= query_pos[:, None])
            scores = (
                jnp.einsum(
                    "rgd,kd->rgk",
                    rows_here[:, head_index],
                    keys_taken,
                    preferred_element_type=jnp.float32,
                )
                * score_scale
            )
            scores = jnp.where(allowed[:, None, :], scores, -jnp.inf)
            peak_row = jnp.max(scores, axis=-1).astype(jnp.bfloat16)
            weights = jnp.exp(scores - peak_row.astype(jnp.float32)[..., None])
            total_row = jnp.sum(weights, axis=-1).astype(jnp.bfloat16)
            mixed = jnp.einsum(
                "rgk,kd->rgd",
                weights.astype(jnp.bfloat16),
                values_taken,
                preferred_element_type=jnp.float32,
            )
            head_outputs.append(
                (mixed / total_row.astype(jnp.float32)[..., None]).astype(jnp.bfloat16)
            )
            head_peaks.append(peak_row)
            head_totals.append(total_row)
        return (jnp.stack(head_outputs, 1), jnp.stack(head_peaks, 1), jnp.stack(head_totals, 1))

    block_ids = jnp.arange(picked.shape[0], dtype=jnp.int32)
    outputs, peaks, totals = lax.map(one_block, (block_ids, picked, usable))
    heads_all = head_count * group_size
    return (
        outputs.reshape(query_tokens, heads_all, HD),
        peaks.reshape(query_tokens, heads_all),
        totals.reshape(query_tokens, heads_all),
    )


def on_device(queries, key_cache, value_cache, blocks, out_weight):
    queries_all = lax.all_gather(queries, "ctx", axis=0, tiled=True)
    local_heads = key_cache.shape[1] // HD
    shard_count = lax.axis_size("ctx")
    blocks_here = key_cache.shape[0] // BLK
    block_lists = lax.dynamic_slice_in_dim(
        blocks, lax.axis_index("kv") * local_heads, local_heads, 1
    )
    here_index = lax.axis_index("ctx")
    shard_first = here_index * blocks_here
    total_keys = shard_count * key_cache.shape[0]
    outputs, peaks, totals = shard_partials(
        queries_all, key_cache, value_cache, block_lists, shard_first, total_keys, local_heads
    )
    received = (
        lax.all_to_all(shortened(outputs[None]), "ctx", split_axis=1, concat_axis=0, tiled=True),
        lax.all_to_all(shortened(peaks[None]), "ctx", split_axis=1, concat_axis=0, tiled=True),
        lax.all_to_all(shortened(totals[None]), "ctx", split_axis=1, concat_axis=0, tiled=True),
    )
    peak_all = received[1].astype(jnp.float32)
    peak_top = jnp.max(peak_all, axis=0)
    weight_all = received[2].astype(jnp.float32) * jnp.exp(peak_all - peak_top)
    summed = jnp.sum(weight_all[..., None] * received[0].astype(jnp.float32), axis=0)
    merged = summed / jnp.sum(weight_all, axis=0)[..., None]
    attended_heads = merged.astype(jnp.bfloat16).reshape(merged.shape[0], -1)
    projected = jnp.dot(
        lax.all_gather(attended_heads, "ctx", axis=0, tiled=True),
        out_weight,
        preferred_element_type=jnp.float32,
    )
    return lax.psum_scatter(projected.astype(jnp.bfloat16), "kv", scatter_dimension=0, tiled=True)


def solution(mesh):
    placed = (P("ctx", "kv"), P("ctx", "kv"), P("ctx", "kv"), P(), P("kv", "ctx"))
    return jax.shard_map(
        on_device, mesh=mesh, in_specs=placed, out_specs=P("kv", "ctx"), check_vma=False
    )
```

profile of v0, /device:TPU:25, one launch (start us, length us, event | category | flops | bytes accessed | tf_op | source)
XLA Modules:
  0.0 417.0 jit_solution(2074537155981065319)
XLA Ops:
  15.3 4.0 reshape.398
  19.3 3.6 copy.105
  23.1 32.5 %all-gather.3.cloned.1.call-done = bf16[1024,2048]{0,1:T(8,128)(2,1)} async-done(((bf16[128,2048]{0,1:T(8,128)(2,1)}), bf16[1024,2048]{0,1:T(8,128)(2,1)}) %all-gather.3.cloned.1.call-update) | async-done | bytes 4194320 | tf_op jit(solution)/shard_map/all_gather | solution.py:90
  55.6 137.5 %while.16 = (s32[]{:T(128)}, bf16[8,128,2,8,128]{4,3,2,1,0:T(8,128)(2,1)}, bf16[8,128,2,8]{1,3,2,0:T(8,128)(2,1)S(1)}, bf16[8,128,2,8]{1,3,2,0:T(8,128)(2,1)S(1)...) while((s32[]{:T(128)}, ...), condition=%wide.region_7.8_spmd.clone.clone, body=%wide.region_2.7_spmd.clone.clone.sunk | while | flops 960972800 | bytes 31813092 | solution.py:80
  55.6 2.9 gather_fusion
  65.0 2.9 gather_fusion.2
  72.8 2.9 gather_fusion
  82.2 2.9 gather_fusion.2
  99.4 2.9 gather_fusion.2
  116.6 2.9 gather_fusion.2
  133.8 2.9 gather_fusion.2
  141.5 2.9 gather_fusion
  151.0 2.9 gather_fusion.2
  168.2 2.9 gather_fusion.2
  175.9 2.9 gather_fusion
  185.3 2.9 gather_fusion.2
  197.3 6.3 %all-to-all-start.1 = ((bf16[8,2,1024]{2,1,0:T(2,128)(2,1)}), bf16[8,2,1024]{2,1,0:T(2,128)(2,1)S(1)}, u32[]{:S(2)}, u32[]{:S(2)}) async-start(bf16[8,2,1024]{2,1,0:T(2,128)(2,1)} %reshape.401), calls=%async_computation.1 | async-start | bytes 65536 | tf_op jit(solution)/shard_map/all_to_all | solution.py:105
  206.6 7.4 %all_to_all.30 = bf16[8,2,1024]{2,1,0:T(2,128)(2,1)S(1)} all-to-all(bf16[8,2,1024]{2,1,0:T(2,128)(2,1)S(1)} %reshape.399), channel_id=1, replica_groups=mesh['kv'=4,'ctx'=8] {'ctx'}, dimensions={0} | all-to-all | bytes 65536 | tf_op jit(solution)/shard_map/all_to_all | solution.py:106
  214.0 7.9 %all-to-all-start.2 = ((bf16[1,1024,16,128]{3,2,0,1:T(8,128)(2,1)}), bf16[1,1024,16,128]{3,2,0,1:T(8,128)(2,1)}, u32[]{:S(2)}, u32[]{:S(2)}) async-start(bf16[1,1024,16,128]{3,2,0,1:T(8,128)(2,1)} %bitcast.183), calls=%async_computation.2 | async-start | bytes 8388608 | tf_op jit(solution)/shard_map/all_to_all | solution.py:104
  223.8 89.5 %all-to-all-done.2 = bf16[1,1024,16,128]{3,2,0,1:T(8,128)(2,1)} async-done(((bf16[1,1024,16,128]{3,2,0,1:T(8,128)(2,1)}), bf16[1,1024,16,128]{3,2,0,1:T(8,128)(2,1)}, u32[]{:S(2)}, u32[]{:S(2)}) %all-to-all-start.2) | async-done | bytes 4194336 | tf_op jit(solution)/shard_map/all_to_all | solution.py:104
  313.3 4.5 %fusion.49 = f32[128,16,128]{2,1,0:T(8,128)S(1)} fusion(bf16[8,128,16,128]{3,2,1,0:T(8,128)(2,1)} %bitcast.37, f32[8,128,16]{2,1,0:T(8,128)S(1)} %copy.112), kind=kLoop, calls=%fused_computation.74 | loop fusion | flops 6029312 | bytes 5308416 | tf_op jit(solution)/shard_map/reduce_sum | solution.py:111
  319.2 46.2 %all-gather.5.cloned.1.call-done = bf16[1024,2048]{1,0:T(8,128)(2,1)} async-done(((bf16[128,2048]{1,0:T(8,128)(2,1)}), bf16[1024,2048]{1,0:T(8,128)(2,1)}) %all-gather.5.cloned.1.call-update) | async-done | bytes 4194320 | tf_op jit(solution)/shard_map/all_gather | solution.py:115
  365.3 9.3 %convolution_convert_fusion = bf16[1024,1024]{1,0:T(8,128)(2,1)} fusion(bf16[1024,2048]{1,0:T(8,128)(2,1)} %all-gather.5.cloned.1.call-done, bf16[2048,1024]{1,0:T(8,128)(2,1)} %param.11), kind=kOutput, calls=%fused_computation.75 | convolution fusion | flops 4296015872 | bytes 10485760 | tf_op jit(solution)/shard_map/dot_general | solution.py:114
  374.6 35.9 %reduce-scatter.2.cloned.1.call-done = bf16[256,1024]{1,0:T(8,128)(2,1)} async-done(((bf16[1024,1024]{1,0:T(8,128)(2,1)}), bf16[256,1024]{1,0:T(8,128)(2,1)}) %reduce-scatter.2.cloned.1.call-update) | async-done | bytes 524304 | tf_op jit(solution)/shard_map/reduce_scatter | solution.py:119
  (313 shorter events, 115.9 us)
Async XLA Ops:
  6.5 2.1 copy-start
  6.5 49.0 %all-gather.3.cloned.1.call-start = ((), (), s32[]{:S(2)}) async-start(), calls=%async_computation.4 | async-start | bytes 4718592 | tf_op jit(solution)/shard_map/all_gather | solution.py:90
  9.2 1.8 copy-start.3
  62.1 1.9 copy-start.1
  68.5 1.9 copy-start.2
  79.2 1.9 copy-start.1
  85.7 1.9 copy-start.2
  96.4 1.9 copy-start.1
  102.9 1.9 copy-start.2
  113.6 1.9 copy-start.1
  120.1 1.9 copy-start.2
  130.8 1.9 copy-start.1
  137.3 1.9 copy-start.2
  148.0 1.9 copy-start.1
  154.5 1.9 copy-start.2
  165.2 1.9 copy-start.1
  171.7 1.9 copy-start.2
  182.3 1.9 copy-start.1
  188.8 1.9 copy-start.2
  197.3 9.3 %all-to-all-start.1 = ((bf16[8,2,1024]{2,1,0:T(2,128)(2,1)}), bf16[8,2,1024]{2,1,0:T(2,128)(2,1)S(1)}, u32[]{:S(2)}, u32[]{:S(2)}) async-start(bf16[8,2,1024]{2,1,0:T(2,128)(2,1)} %reshape.401), calls=%async_computation.1 | async-start | bytes 65536 | tf_op jit(solution)/shard_map/all_to_all | solution.py:105
  214.0 99.3 %all-to-all-start.2 = ((bf16[1,1024,16,128]{3,2,0,1:T(8,128)(2,1)}), bf16[1,1024,16,128]{3,2,0,1:T(8,128)(2,1)}, u32[]{:S(2)}, u32[]{:S(2)}) async-start(bf16[1,1024,16,128]{3,2,0,1:T(8,128)(2,1)} %bitcast.183), calls=%async_computation.2 | async-start | bytes 8388608 | tf_op jit(solution)/shard_map/all_to_all | solution.py:104
  221.9 143.4 %all-gather.5.cloned.1.call-start = ((), (), s32[]{:S(2)}) async-start(), calls=%async_computation.5 | async-start | bytes 4718592 | tf_op jit(solution)/shard_map/all_gather | solution.py:115
  319.1 91.4 %reduce-scatter.2.cloned.1.call-start = ((), (), s32[]{:S(2)}) async-start(), calls=%async_computation.6 | async-start | bytes 2621440 | tf_op jit(solution)/shard_map/reduce_scatter | solution.py:119
Sparse Core Ops, SparseCore 0:
  8.9 46.5 all-gather.2
  319.2 46.0 all-gather.4
  374.8 35.6 reduce-scatter.1
where the time goes:
time: 420 us; the launch traced here: 417 us
  waiting for transfers between devices  204 us (49%)
  local copies, waits for them, and re-layouts  102 us (24%)
  matrix products  41 us (10%)
  other arithmetic  29 us (7%)
  starting transfers between devices  14.2 us (3%)
  between operations  13.3 us (3%)
  blocking collectives  7.37 us (2%)
  loops' own time  6.25 us (1%)
    all_to_all x1, waiting for transfers between devices, on_device(): lax.all_to_all(shortened(outputs[None]), 'ctx', split_axis=1, concat_axis...  89.5 us
    all_gather x1, waiting for transfers between devices, on_device(): lax.all_gather(attended_heads, 'ctx', axis=0, tiled=True)  46.2 us
    gather x16, local copies, waits for them, and re-layouts, one_block(): value_blocks[chosen, :, head_index, :].reshape(MOST * BLK, HD)  46.1 us
    reduce_scatter x1, waiting for transfers between devices, on_device(): lax.psum_scatter(projected.astype(jnp.bfloat16), 'kv', scatter_dimension=...  35.9 us
    all_gather x1, waiting for transfers between devices, on_device(): queries_all = lax.all_gather(queries, 'ctx', axis=0, tiled=True)  32.5 us
    dot_general x16, matrix products, one_block(): jnp.einsum('rgk,kd->rgd', weights.astype(jnp.bfloat16), values_taken, pre...  16.5 us
    reduce_sum x16, other arithmetic, one_block(): total_row = jnp.sum(weights, axis=-1).astype(jnp.bfloat16)  15.3 us
    dot_general x16, matrix products, one_block(): jnp.einsum('rgd,kd->rgk', rows_here[:, head_index], keys_taken, preferred...  15.2 us
  transfers between devices with their start and end apart: 5, of which 4 were waited for; matrix products, arithmetic and copies ran while one was open for 5% of the time, Pallas kernels for 0%

commit v1 on v0

v1 whole, which is shorter than its diff:
```python
import functools
import math

import jax
import jax.numpy as jnp
from jax import lax
from jax.experimental import pallas as pl
from jax.experimental.pallas import tpu as pltpu
from jax.sharding import PartitionSpec as P

HD = 128
BLK = 128
MOST = 7
COUNTS = (1, 3, 5, 7)
LOG2E = math.log2(math.e)


def attend_kernel(diag_first, heads, picked, counts, last, q_ref, k_ref, v_ref, o_ref, lse_ref):
    head_index, block_index = pl.program_id(0), pl.program_id(1)
    count = counts[block_index, head_index]
    on_diagonal = last[block_index, head_index] == diag_first + block_index
    rows = lax.broadcasted_iota(jnp.int32, (2 * BLK, BLK), 0) % BLK
    columns = lax.broadcasted_iota(jnp.int32, (2 * BLK, BLK), 1)
    lanes = lax.broadcasted_iota(jnp.int32, (BLK, BLK), 1)
    hidden = (columns > rows) & on_diagonal
    scale = LOG2E / math.sqrt(HD)

    def with_count(many):
        places = [
            pl.ds(pl.multiple_of(picked[block_index, head_index, slot] * BLK, BLK), BLK)
            for slot in range(many)
        ]
        keys = jnp.concatenate([k_ref[place, :] for place in places], 0)
        values = jnp.concatenate([v_ref[place, :] for place in places], 0)
        stats = jnp.zeros((BLK, BLK), jnp.float32)
        for pair in range(heads // 2):
            at = [slice((2 * pair + i) * HD, (2 * pair + i + 1) * HD) for i in range(2)]
            rows_now = jnp.concatenate([q_ref[:, a] for a in at], 0)
            scores = lax.dot_general(
                rows_now, keys, (((1,), (1,)), ((), ())), preferred_element_type=jnp.float32
            )
            tail = jnp.where(hidden, -jnp.inf, scores[:, (many - 1) * BLK :])
            scores = jnp.concatenate([scores[:, : (many - 1) * BLK], tail], 1) if many > 1 else tail
            peak = jnp.max(scores, axis=1, keepdims=True) * scale
            weights = jnp.exp2(scores * scale - peak)
            total = jnp.sum(weights, axis=1, keepdims=True)
            mixed = jnp.dot(
                weights.astype(jnp.bfloat16), values, preferred_element_type=jnp.float32
            )
            mixed = (mixed / total).astype(jnp.bfloat16)
            lse = peak + jnp.log2(total)
            for i in range(2):
                part = slice(i * BLK, (i + 1) * BLK)
                o_ref[:, at[i]] = mixed[part]
                stats = jnp.where(lanes == 2 * pair + i, lse[part], stats)
        lse_ref[0] = stats.T[:heads]

    for many in COUNTS:
        pl.when(count == many)(functools.partial(with_count, many))


def attend(queries_all, keys, values, picked, counts, last, diag_first):
    tokens, columns = queries_all.shape
    head_count = keys.shape[1] // HD
    group = columns // (head_count * HD)
    query_blocks = tokens // BLK
    spec = pltpu.PrefetchScalarGridSpec(
        num_scalar_prefetch=3,
        grid=(head_count, query_blocks),
        in_specs=[
            pl.BlockSpec((BLK, group * HD), lambda h, b, *_: (b, h)),
            pl.BlockSpec((keys.shape[0], HD), lambda h, b, *_: (0, h)),
            pl.BlockSpec((keys.shape[0], HD), lambda h, b, *_: (0, h)),
        ],
        out_specs=[
            pl.BlockSpec((BLK, group * HD), lambda h, b, *_: (b, h)),
            pl.BlockSpec((1, group, BLK), lambda h, b, *_: (b, h, 0)),
        ],
    )
    return pl.pallas_call(
        functools.partial(attend_kernel, diag_first, group),
        grid_spec=spec,
        out_shape=[
            jax.ShapeDtypeStruct((tokens, columns), jnp.bfloat16),
            jax.ShapeDtypeStruct((query_blocks, head_count * group, BLK), jnp.float32),
        ],
        compiler_params=pltpu.CompilerParams(vmem_limit_bytes=40 * 2**20),
        name="attend",
    )(picked, counts, last, queries_all, keys, values)


def choose(blocks, head_count, shard_first, blocks_here):
    lists = lax.dynamic_slice_in_dim(blocks, lax.axis_index("kv") * head_count, head_count, 1)
    local = lists - shard_first
    below = jnp.sum((local < 0).astype(jnp.int32), axis=-1)
    counts = jnp.sum(((local >= 0) & (local < blocks_here)).astype(jnp.int32), axis=-1)
    slots = jnp.arange(MOST, dtype=jnp.int32)
    places = jnp.arange(blocks.shape[-1], dtype=jnp.int32)
    here = places == (below[..., None] + slots)[..., None]
    picked = jnp.sum(jnp.where(here, local[:, :, None, :], 0), axis=-1)
    picked = jnp.clip(picked, 0, blocks_here - 1)
    last = jnp.sum(jnp.where(slots == (counts - 1)[..., None], picked, 0), axis=-1)
    return picked, counts, last + shard_first


def on_device(queries, key_cache, value_cache, blocks, out_weight):
    head_count = key_cache.shape[1] // HD
    shards = lax.axis_size("ctx")
    blocks_here = key_cache.shape[0] // BLK
    tokens_each = queries.shape[0]
    tokens = tokens_each * shards
    shard_first = lax.axis_index("ctx") * blocks_here
    picked, counts, last = choose(blocks, head_count, shard_first, blocks_here)
    queries_all = lax.all_gather(queries, "ctx", axis=0, tiled=True)
    diag_first = shards * blocks_here - tokens // BLK
    outputs, lse = attend(
        queries_all, key_cache, value_cache, picked, counts, last, diag_first
    )
    outputs = lax.all_to_all(
        outputs.reshape(shards, tokens_each, -1), "ctx", split_axis=0, concat_axis=0, tiled=True
    )
    heads = lse.shape[1]
    lse = lse.transpose(0, 2, 1).reshape(shards, tokens_each, heads)
    lse = lax.all_to_all(lse, "ctx", split_axis=0, concat_axis=0, tiled=True)
    shares = jnp.exp2(lse - jnp.max(lse, axis=0))
    shares = shares / jnp.sum(shares, axis=0)
    outputs = outputs.reshape(shards, tokens_each, heads, HD).astype(jnp.float32)
    merged = jnp.sum(shares[..., None] * outputs, axis=0).astype(jnp.bfloat16)
    merged = merged.reshape(tokens_each, heads * HD)
    projected = jnp.dot(
        lax.all_gather(merged, "ctx", axis=0, tiled=True),
        out_weight,
        preferred_element_type=jnp.float32,
    )
    return lax.psum_scatter(projected.astype(jnp.bfloat16), "kv", scatter_dimension=0, tiled=True)


def solution(mesh):
    placed = (P("ctx", "kv"), P("ctx", "kv"), P("ctx", "kv"), P(), P("kv", "ctx"))
    return jax.shard_map(
        on_device, mesh=mesh, in_specs=placed, out_specs=P("kv", "ctx"), check_vma=False
    )
```

time: 420 us -> 313 us (0.75)
  local copies, waits for them, and re-layouts: 102 us -> 21.7 us
  Pallas kernels: 0 us -> 36.8 us
  matrix products: 41 us -> 9.28 us
  other arithmetic: 29 us -> 7.77 us
  loops' own time: 6.25 us -> 0 us
  starting transfers between devices: 14.2 us -> 8.03 us
    gather x35 -> x0, local copies, waits for them, and re-layouts: 57.9 us -> none  [the longest x16 46.1 us: one_block(): value_blocks[chosen, :, head_index, :].reshape(MOST * BLK, HD)]
    pallas_call x0 -> x1, Pallas kernels: none -> 36.8 us  [attend(): pl.pallas_call(functools.partial(attend_kernel, diag_first, group), grid_...]
    dot_general x33 -> x1, matrix products: 41 us -> 9.28 us  [on_device(): jnp.dot(lax.all_gather(merged, 'ctx', axis=0, tiled=True), out_weight, pr...]
    all_gather x1, waiting for transfers between devices: 32.5 us -> 46.9 us  [on_device(): queries_all = lax.all_gather(queries, 'ctx', axis=0, tiled=True)]
    dynamic_slice x33 -> x1, local copies, waits for them, and re-layouts: 13.9 us -> 0.01 us  [choose(): lax.dynamic_slice_in_dim(blocks, lax.axis_index('kv') * head_count, head_...]
    mul x1 -> x2, local copies, waits for them, and re-layouts: 0.2 us -> 13.9 us  [on_device(): merged = jnp.sum(shares[..., None] * outputs, axis=0).astype(jnp.bfloat16)]
    reduce_sum x19 -> x5, other arithmetic: 20 us -> 7.72 us  [the longest x1 6.88 us: on_device(): merged = jnp.sum(shares[..., None] * outputs, axis=0).astype(jnp.bfloat16)]
    all_to_all x2 -> x1, waiting for transfers between devices: 89.5 us -> 77.3 us  [on_device(): lax.all_to_all(outputs.reshape(shards, tokens_each, -1), 'ctx', split_axi...]
  transfers between devices with their start and end apart: 5 -> 4, of which waited for: 4 -> 4; matrix products, arithmetic and copies ran while one was open for 5% -> 5% of each run, Pallas kernels for 0% -> 0%
where the time goes in v1:
time: 313 us; the launch traced here: 311 us
  waiting for transfers between devices  207 us (66%)
  Pallas kernels  36.8 us (12%)
  local copies, waits for them, and re-layouts  21.7 us (7%)
  between operations  13.2 us (4%)
  matrix products  9.28 us (3%)
  starting transfers between devices  8.03 us (3%)
  other arithmetic  7.77 us (2%)
  blocking collectives  7.2 us (2%)
    all_to_all x1, waiting for transfers between devices, on_device(): lax.all_to_all(outputs.reshape(shards, tokens_each, -1), 'ctx', split_axi...  77.3 us
    all_gather x1, waiting for transfers between devices, on_device(): queries_all = lax.all_gather(queries, 'ctx', axis=0, tiled=True)  46.9 us
    all_gather x1, waiting for transfers between devices, on_device(): lax.all_gather(merged, 'ctx', axis=0, tiled=True)  46.1 us
    pallas_call x1, Pallas kernels, attend(): pl.pallas_call(functools.partial(attend_kernel, diag_first, group), grid_...  36.8 us
    reduce_scatter x1, waiting for transfers between devices, on_device(): lax.psum_scatter(projected.astype(jnp.bfloat16), 'kv', scatter_dimension=...  35.9 us
    mul x2, local copies, waits for them, and re-layouts, on_device(): merged = jnp.sum(shares[..., None] * outputs, axis=0).astype(jnp.bfloat16)  13.9 us
    dot_general x1, matrix products, on_device(): jnp.dot(lax.all_gather(merged, 'ctx', axis=0, tiled=True), out_weight, pr...  9.28 us
    all_to_all x1, starting transfers between devices, on_device(): lax.all_to_all(outputs.reshape(shards, tokens_each, -1), 'ctx', split_axi...  7.81 us
  transfers between devices with their start and end apart: 4, of which 4 were waited for; matrix products, arithmetic and copies ran while one was open for 5% of the time, Pallas kernels for 0%

profile of v1, /device:TPU:25, one launch (start us, length us, event | category | flops | bytes accessed | tf_op | source)
XLA Modules:
  0.0 310.8 jit_solution(10063991048807550804)
XLA Ops:
  6.5 0.7 all-gather.3.cloned.1.call-update
  7.3 0.1 convert_reduce_fusion
  7.5 0.1 copy.24.counts
  7.5 0.1 copy.23
  7.6 0.4 select_reduce_fusion
  8.0 0.1 copy.22
  8.1 0.3 fusion.2
  8.4 46.9 %all-gather.3.cloned.1.call-done.q_ref = bf16[1024,2048]{1,0:T(8,128)(2,1)} async-done(((bf16[128,2048]{1,0:T(8,128)(2,1)}), bf16[1024,2048]{1,0:T(8,128)(2,1)}) %all-gather.3.cloned.1.call-update) | async-done | bytes 4194320 | tf_op jit(solution)/shard_map/all_gather | solution.py:114
  55.3 2.2 copy-done.1
  57.5 1.6 copy-done.3
  59.1 1.6 copy-done.4
  60.7 36.8 %attend.1 = (bf16[1024,2048]{1,0:T(8,128)(2,1)S(1)}, f32[8,16,128]{2,1,0:T(8,128)S(1)}) custom-call(s32[8,2,7]{2,1,0:T(2,128)S(1)} %get-tuple-element.13.picked, s32[8,2]{1,0:T(8,128)S(1)} %copy.24.counts, s32[8,2]{1,0:T(8,128)S(1)} %broadcast_add_fusion.last, bf16[1024,2048]{1,0:T(8,128)(2,1)S(1)} %copy-done.1, bf16[4096,256]{1,0:T(8,128)(2,1)S(1)} %copy-done.3, ...), custom_call_target="tpu_custom_call" | custom-call | tf_op jit(solution)/shard_map/attend/pallas_call | solution.py:80
  97.5 2.0 copy-done.2
  99.4 7.2 %all_to_all.10 = f32[8,128,16]{1,2,0:T(8,128)S(1)} all-to-all(f32[8,128,16]{1,2,0:T(8,128)S(1)} %bitcast.7), channel_id=1, replica_groups=mesh['kv'=4,'ctx'=8] {'ctx'}, dimensions={0} | all-to-all | bytes 131072 | tf_op jit(solution)/shard_map/all_to_all | solution.py:124
  106.6 7.8 %all-to-all-start.1 = ((bf16[8,128,2048]{2,1,0:T(8,128)(2,1)}), bf16[8,128,2048]{2,1,0:T(8,128)(2,1)}, u32[]{:S(2)}, u32[]{:S(2)}) async-start(bf16[8,128,2048]{2,1,0:T(8,128)(2,1)} %bitcast.6), calls=%async_computation.1 | async-start | bytes 8388608 | tf_op jit(solution)/shard_map/all_to_all | solution.py:119
  114.5 0.2 copy.25
  114.7 4.6 %mul.19 = f32[8,128,16,128]{3,2,1,0:T(8,128)} broadcast(f32[8,128,16]{2,1,0:T(8,128)S(1)} %copy.25), dimensions={0,1,2} | broadcast | bytes 8454144 | tf_op jit(solution)/shard_map/mul | solution.py:128
  119.3 9.3 %mul.20 = f32[8,128,2048]{2,1,0:T(8,128)} reshape(f32[8,128,16,128]{3,2,1,0:T(8,128)} %mul.19) | data formatting | bytes 16777216 | tf_op jit(solution)/shard_map/mul | solution.py:128
  128.6 77.3 %all-to-all-done.1 = bf16[8,128,2048]{2,1,0:T(8,128)(2,1)} async-done(((bf16[8,128,2048]{2,1,0:T(8,128)(2,1)}), bf16[8,128,2048]{2,1,0:T(8,128)(2,1)}, u32[]{:S(2)}, u32[]{:S(2)}) %all-to-all-start.1) | async-done | bytes 4194336 | tf_op jit(solution)/shard_map/all_to_all | solution.py:119
  205.9 6.9 %multiply_reduce_fusion = bf16[128,2048]{1,0:T(8,128)(2,1)} fusion(f32[8,128,2048]{2,1,0:T(8,128)} %mul.20, bf16[8,128,2048]{2,1,0:T(8,128)(2,1)} %all-to-all-done.1), kind=kLoop, calls=%fused_computation | loop fusion | flops 6029312 | bytes 13107200 | tf_op jit(solution)/shard_map/reduce_sum | solution.py:128
  212.8 0.2 reduce-scatter.2.cloned.1.call-start
  213.0 46.1 %all-gather.5.cloned.1.call-done = bf16[1024,2048]{1,0:T(8,128)(2,1)} async-done(((bf16[128,2048]{1,0:T(8,128)(2,1)}), bf16[1024,2048]{1,0:T(8,128)(2,1)}) %all-gather.5.cloned.1.call-update) | async-done | bytes 4194320 | tf_op jit(solution)/shard_map/all_gather | solution.py:131
  259.2 9.3 %convolution_convert_fusion = bf16[1024,1024]{1,0:T(8,128)(2,1)} fusion(bf16[1024,2048]{1,0:T(8,128)(2,1)} %all-gather.5.cloned.1.call-done, bf16[2048,1024]{1,0:T(8,128)(2,1)} %param.9), kind=kOutput, calls=%fused_computation.1 | convolution fusion | flops 4296015872 | bytes 10485760 | tf_op jit(solution)/shard_map/dot_general | solution.py:130
  268.5 35.9 %reduce-scatter.2.cloned.1.call-done = bf16[256,1024]{1,0:T(8,128)(2,1)} async-done(((bf16[1024,1024]{1,0:T(8,128)(2,1)}), bf16[256,1024]{1,0:T(8,128)(2,1)}) %reduce-scatter.2.cloned.1.call-update) | async-done | bytes 524304 | tf_op jit(solution)/shard_map/reduce_scatter | solution.py:135
  (17 shorter events, 0.2 us)
Async XLA Ops:
  6.5 0.8 copy-start
  6.5 48.8 %all-gather.3.cloned.1.call-start = ((), (), s32[]{:S(2)}) async-start(), calls=%async_computation.3 | async-start | bytes 4718592 | tf_op jit(solution)/shard_map/all_gather | solution.py:114
  55.3 2.2 copy-start.1
  57.5 1.6 copy-start.3
  59.1 1.6 copy-start.4
  97.5 2.0 copy-start.2
  106.6 99.2 %all-to-all-start.1 = ((bf16[8,128,2048]{2,1,0:T(8,128)(2,1)}), bf16[8,128,2048]{2,1,0:T(8,128)(2,1)}, u32[]{:S(2)}, u32[]{:S(2)}) async-start(bf16[8,128,2048]{2,1,0:T(8,128)(2,1)} %bitcast.6), calls=%async_computation.1 | async-start | bytes 8388608 | tf_op jit(solution)/shard_map/all_to_all | solution.py:119
  114.5 144.7 %all-gather.5.cloned.1.call-start = ((), (), s32[]{:S(2)}) async-start(), calls=%async_computation.4 | async-start | bytes 4718592 | tf_op jit(solution)/shard_map/all_gather | solution.py:131
  212.8 91.5 %reduce-scatter.2.cloned.1.call-start = ((), (), s32[]{:S(2)}) async-start(), calls=%async_computation.5 | async-start | bytes 2621440 | tf_op jit(solution)/shard_map/reduce_scatter | solution.py:135
Sparse Core Ops, SparseCore 0:
  9.0 46.3 all-gather.2
  212.9 46.1 all-gather.4
  268.6 35.6 reduce-scatter.1

commit v2 on v1

v2 whole, which is shorter than its diff:
```python
import math

import jax
import jax.numpy as jnp
from jax import lax
from jax.experimental import pallas as pl
from jax.experimental.pallas import tpu as pltpu
from jax.sharding import PartitionSpec as P

HD = 128
BLK = 128
MOST = 7
LOG2E = math.log2(math.e)
MESH = pl.DeviceIdType.MESH


def layer_kernel(
    shards,
    groups,
    picked,
    biases,
    q_ref,
    k_ref,
    v_ref,
    w_hbm,
    out_ref,
    q_all,
    part,
    part_lse,
    pair_in,
    pair_lse,
    stage,
    stage_lse,
    chip_in,
    chip_lse,
    merged_all,
    weight,
    projected,
    group_in,
    q_send,
    q_recv,
    m_send,
    m_recv,
    pair_send,
    pair_recv,
    pair_lse_send,
    pair_lse_recv,
    chip_send,
    chip_recv,
    chip_lse_send,
    chip_lse_recv,
    group_send,
    group_recv,
    w_sem,
):
    me, group_me = lax.axis_index("ctx"), lax.axis_index("kv")
    chips = shards // 2
    chip, core = me // 2, me % 2
    partner = chip * 2 + 1 - core
    tokens = q_ref.shape[0]
    columns = q_ref.shape[1]
    heads = columns // HD
    lists = k_ref.shape[2] // HD
    per_list = heads // lists
    per_group = shards // groups
    scale = LOG2E / math.sqrt(HD)

    weight_copy = pltpu.make_async_copy(w_hbm, weight, w_sem)
    weight_copy.start()

    barrier = pltpu.get_barrier_semaphore()
    pl.semaphore_signal(barrier, inc=1, device_id={"ctx": partner}, device_id_type=MESH)
    for step in range(1, chips):
        other = lax.rem(chip + step, chips) * 2 + core
        pl.semaphore_signal(barrier, inc=1, device_id={"ctx": other}, device_id_type=MESH)
    for step in range(1, groups):
        other = lax.rem(group_me + step, groups)
        pl.semaphore_signal(barrier, inc=1, device_id={"kv": other}, device_id_type=MESH)
    pl.semaphore_wait(barrier, chips + groups - 1)

    def remote(source, target, send, recv, where):
        return pltpu.make_async_remote_copy(
            src_ref=source,
            dst_ref=target,
            send_sem=send,
            recv_sem=recv,
            device_id=where,
            device_id_type=MESH,
        )

    def along(buffer, send, recv, slot, way):
        target = {0: me + 2, 1: me - 2, 2: partner}[way]
        return remote(
            buffer.at[slot], buffer.at[slot], send.at[way, slot], recv.at[slot], {"ctx": target}
        )

    def spread(buffer, send, recv, step):
        def pass_on(slot, way, allowed):
            @pl.when(allowed)
            def _():
                along(buffer, send, recv, slot, way).start()

        low, high = chip - step, chip + step

        @pl.when(low >= 0)
        def _():
            slot = low * 2 + core

            @pl.when(step > 0)
            def _():
                along(buffer, send, recv, slot, 0).wait_recv()

            pass_on(slot, 0, chip + 1 < chips)
            pass_on(slot, 2, step >= 0)

        @pl.when(high < chips)
        def _():
            slot = high * 2 + core

            @pl.when(step > 0)
            def _():
                along(buffer, send, recv, slot, 1).wait_recv()

            pass_on(slot, 1, chip >= 1)
            pass_on(slot, 2, step > 0)

    def finish_spread(buffer, send, recv):
        def one(at, carry):
            slot = at * 2 + core

            @pl.when((at <= chip) & (chip + 1 < chips))
            def _():
                along(buffer, send, recv, slot, 0).wait_send()

            @pl.when((at >= chip) & (chip >= 1))
            def _():
                along(buffer, send, recv, slot, 1).wait_send()

            along(buffer, send, recv, slot, 2).wait_send()
            return carry

        lax.fori_loop(0, chips, one, 0)

    def pair_copies(at):
        slot = at * 2 + 1 - core
        where = {"ctx": partner}
        return (
            remote(part.at[slot], pair_in.at[at], pair_send.at[at], pair_recv.at[at], where),
            remote(
                part_lse.at[slot],
                pair_lse.at[at],
                pair_lse_send.at[at],
                pair_lse_recv.at[at],
                where,
            ),
        )

    def chip_copies(source, target):
        where = {"ctx": target * 2 + core}
        return (
            remote(
                stage.at[target],
                chip_in.at[source],
                chip_send.at[target],
                chip_recv.at[source],
                where,
            ),
            remote(
                stage_lse.at[target],
                chip_lse.at[source],
                chip_lse_send.at[target],
                chip_lse_recv.at[source],
                where,
            ),
        )

    def group_copy(slot, source):
        inside = slot % per_group
        return remote(
            projected.at[slot],
            group_in.at[source, inside],
            group_send.at[slot],
            group_recv.at[source, inside],
            {"kv": slot // per_group},
        )

    def attend(slot):
        first = slot * tokens
        block_index, offset = first // BLK, first % BLK
        stack = max(1, min(per_list, 2 * BLK // tokens))
        rows = lax.broadcasted_iota(jnp.int32, (stack * tokens, BLK), 0) % tokens + offset
        places = lax.broadcasted_iota(jnp.int32, (stack * tokens, BLK), 1)
        lanes = lax.broadcasted_iota(jnp.int32, (tokens, BLK), 1)
        stats = jnp.zeros((tokens, BLK), jnp.float32)
        for index in range(lists):
            chosen = [picked[block_index, index, at] for at in range(MOST)]
            bias = [biases[block_index, index, at] for at in range(MOST)]
            causal = jnp.where(places > rows, bias[0], 0.0)
            here = slice(index * HD, (index + 1) * HD)
            keys = jnp.concatenate([k_ref[one, :, here] for one in chosen], 0)
            values = jnp.concatenate([v_ref[one, :, here] for one in chosen], 0)
            for begin in range(index * per_list, (index + 1) * per_list, stack):
                at = [slice(g * HD, (g + 1) * HD) for g in range(begin, begin + stack)]
                queries = jnp.concatenate([q_all[slot, :, a] for a in at], 0)
                scores = lax.dot_general(
                    queries, keys, (((1,), (1,)), ((), ())), preferred_element_type=jnp.float32
                )
                pieces = [scores[:, :BLK] + causal]
                for s in range(1, MOST):
                    pieces.append(scores[:, s * BLK : (s + 1) * BLK] + bias[s])
                scores = jnp.concatenate(pieces, 1)
                peak = jnp.max(scores, axis=1, keepdims=True) * scale
                weights = jnp.exp2(scores * scale - peak)
                total = jnp.sum(weights, axis=1, keepdims=True)
                mixed = jnp.dot(
                    weights.astype(jnp.bfloat16), values, preferred_element_type=jnp.float32
                )
                mixed = (mixed / total).astype(jnp.bfloat16)
                lse = peak + jnp.log2(total)
                for i in range(stack):
                    mine = slice(i * tokens, (i + 1) * tokens)
                    part[slot, :, at[i]] = mixed[mine]
                    stats = jnp.where(lanes == begin + i, lse[mine], stats)
        part_lse[slot] = stats.T[:heads]

    def merge_pair(at):
        slot = at * 2 + core
        for copy in pair_copies(at):
            copy.wait_recv()
        own, other = part_lse[slot], pair_lse[at]
        top = jnp.maximum(own, other)
        own, other = jnp.exp2(own - top), jnp.exp2(other - top)
        total = own + other
        joint = top + jnp.log2(total)
        own, other = (own / total).T, (other / total).T

        def store(to, to_lse, place):
            to_lse[place] = joint
            for g in range(heads):
                a = slice(g * HD, (g + 1) * HD)
                both = own[:, g : g + 1] * part[slot, :, a].astype(jnp.float32)
                both += other[:, g : g + 1] * pair_in[at, :, a].astype(jnp.float32)
                to[place, :, a] = both.astype(jnp.bfloat16)

        @pl.when(at == chip)
        def _():
            store(chip_in, chip_lse, chip)

        @pl.when(at != chip)
        def _():
            store(stage, stage_lse, at)
            for copy in chip_copies(chip, at):
                copy.start()

    def each(step, visit):
        def one(index, carry):
            side, own_core = index % 2, index // 2
            at = jnp.where(side == 0, chip - step, chip + step)
            valid = (at >= 0) & (at < chips) & ((step > 0) | (side == 0))

            @pl.when(valid)
            def _():
                visit(at, own_core)

            return carry

        return one

    q_all[me] = q_ref[...]

    def attend_step(step, carry):
        spread(q_all, q_send, q_recv, step)

        def visit(at, own_core):
            slot = at * 2 + jnp.where(own_core == 1, core, 1 - core)

            @pl.when(own_core == 0)
            def _():
                along(q_all, q_send, q_recv, slot, 2).wait_recv()

            attend(slot)

            @pl.when(own_core == 0)
            def _():
                for copy in pair_copies(at):
                    copy.start()

        lax.fori_loop(0, 4, each(step, visit), 0)
        lax.fori_loop(0, 2, each(step, lambda at, own_core: merge_pair(at)), 0)
        return carry

    lax.fori_loop(0, chips, attend_step, 0)

    def receive(step, carry):
        source = lax.rem(chip + step, chips)
        for copy in chip_copies(source, chip):
            copy.wait_recv()
        return carry

    lax.fori_loop(1, chips, receive, 0)
    top = chip_lse[0]
    for c in range(1, chips):
        top = jnp.maximum(top, chip_lse[c])
    shares = [jnp.exp2(chip_lse[c] - top) for c in range(chips)]
    total = shares[0]
    for c in range(1, chips):
        total = total + shares[c]
    shares = [(share / total).T for share in shares]
    for g in range(heads):
        a = slice(g * HD, (g + 1) * HD)
        summed = shares[0][:, g : g + 1] * chip_in[0, :, a].astype(jnp.float32)
        for c in range(1, chips):
            summed += shares[c][:, g : g + 1] * chip_in[c, :, a].astype(jnp.float32)
        merged_all[me, :, a] = summed.astype(jnp.bfloat16)

    weight_copy.wait()

    def project_step(step, carry):
        spread(merged_all, m_send, m_recv, step)

        def visit(at, own_core):
            slot = at * 2 + jnp.where(own_core == 1, 1 - core, core)

            @pl.when(own_core == 1)
            def _():
                along(merged_all, m_send, m_recv, slot, 2).wait_recv()

            projected[slot] = jnp.dot(
                merged_all[slot], weight[...], preferred_element_type=jnp.float32
            ).astype(jnp.bfloat16)

            @pl.when(slot // per_group != group_me)
            def _():
                group_copy(slot, group_me).start()

        lax.fori_loop(0, 4, each(step, visit), 0)
        return carry

    lax.fori_loop(0, chips, project_step, 0)

    def gather_groups(inside, carry):
        total = projected[group_me * per_group + inside].astype(jnp.float32)
        for step in range(1, groups):
            source = lax.rem(group_me + step, groups)
            group_copy(group_me * per_group + inside, source).wait_recv()
            total += group_in[source, inside].astype(jnp.float32)
        out_ref[pl.ds(pl.multiple_of(inside * tokens, tokens), tokens), :] = total.astype(
            out_ref.dtype
        )
        return carry

    lax.fori_loop(0, per_group, gather_groups, 0)

    finish_spread(q_all, q_send, q_recv)
    finish_spread(merged_all, m_send, m_recv)

    def finish_chips(at, carry):
        for copy in pair_copies(at):
            copy.wait_send()

        @pl.when(at != chip)
        def _():
            for copy in chip_copies(chip, at):
                copy.wait_send()

        return carry

    lax.fori_loop(0, chips, finish_chips, 0)

    def finish_groups(slot, carry):
        @pl.when(slot // per_group != group_me)
        def _():
            group_copy(slot, group_me).wait_send()

        return carry

    lax.fori_loop(0, shards, finish_groups, 0)


def layer(queries, keys, values, picked, biases, out_weight, shards, groups):
    tokens, columns = queries.shape
    heads = columns // HD
    chips = shards // 2
    wide = out_weight.shape[1]
    per_group = shards // groups
    half, full = jnp.bfloat16, jnp.float32
    dma = pltpu.SemaphoreType.DMA
    smem = pl.BlockSpec(memory_space=pltpu.SMEM)
    vmem = pl.BlockSpec(memory_space=pltpu.VMEM)

    def body(*refs):
        layer_kernel(shards, groups, *refs)

    return pl.pallas_call(
        body,
        in_specs=[smem] * 2 + [vmem] * 3 + [pl.BlockSpec(memory_space=pl.ANY)],
        out_specs=vmem,
        out_shape=jax.ShapeDtypeStruct((per_group * tokens, wide), half),
        scratch_shapes=[
            pltpu.VMEM((shards, tokens, columns), half),
            pltpu.VMEM((shards, tokens, columns), half),
            pltpu.VMEM((shards, heads, tokens), full),
            pltpu.VMEM((chips, tokens, columns), half),
            pltpu.VMEM((chips, heads, tokens), full),
            pltpu.VMEM((chips, tokens, columns), half),
            pltpu.VMEM((chips, heads, tokens), full),
            pltpu.VMEM((chips, tokens, columns), half),
            pltpu.VMEM((chips, heads, tokens), full),
            pltpu.VMEM((shards, tokens, columns), half),
            pltpu.VMEM(out_weight.shape, half),
            pltpu.VMEM((shards, tokens, wide), half),
            pltpu.VMEM((groups, per_group, tokens, wide), half),
            dma((3, shards)),
            dma((shards,)),
            dma((3, shards)),
            dma((shards,)),
            dma((chips,)),
            dma((chips,)),
            dma((chips,)),
            dma((chips,)),
            dma((chips,)),
            dma((chips,)),
            dma((chips,)),
            dma((chips,)),
            dma((shards,)),
            dma((groups, per_group)),
            dma,
        ],
        compiler_params=pltpu.CompilerParams(
            collective_id=0, has_side_effects=True, vmem_limit_bytes=56 * 2**20
        ),
        name="layer",
    )(picked, biases, queries, keys, values, out_weight)


def choose(blocks, head_count, shard_first, blocks_here, diag_first):
    lists = lax.dynamic_slice_in_dim(blocks, lax.axis_index("kv") * head_count, head_count, 1)
    local = lists - shard_first
    below = jnp.sum((local < 0).astype(jnp.int32), axis=-1)
    counts = jnp.sum(((local >= 0) & (local < blocks_here)).astype(jnp.int32), axis=-1)
    slots = jnp.arange(MOST, dtype=jnp.int32)
    places = jnp.arange(blocks.shape[-1], dtype=jnp.int32)
    here = places == ((below + counts - 1)[..., None] - slots)[..., None]
    picked = jnp.sum(jnp.where(here, local[:, :, None, :], 0), axis=-1)
    picked = jnp.clip(picked, 0, blocks_here - 1)
    query_block = jnp.arange(blocks.shape[0], dtype=jnp.int32)[:, None]
    diagonal = picked[..., 0] + shard_first == diag_first + query_block
    barred = jnp.where(slots == 0, diagonal[..., None], slots >= counts[..., None])
    return picked, jnp.where(barred, -jnp.inf, 0.0).astype(jnp.float32)


def on_device(queries, key_cache, value_cache, blocks, out_weight):
    head_count = key_cache.shape[1] // HD
    shards, groups = lax.axis_size("ctx"), lax.axis_size("kv")
    blocks_here = key_cache.shape[0] // BLK
    shard_first = lax.axis_index("ctx") * blocks_here
    diag_first = shards * blocks_here - queries.shape[0] * shards // BLK
    picked, biases = choose(blocks, head_count, shard_first, blocks_here, diag_first)
    keys = key_cache.reshape(blocks_here, BLK, -1)
    values = value_cache.reshape(blocks_here, BLK, -1)
    return layer(queries, keys, values, picked, biases, out_weight, shards, groups)


def solution(mesh):
    placed = (P("ctx", "kv"), P("ctx", "kv"), P("ctx", "kv"), P(), P("kv", "ctx"))
    return jax.shard_map(
        on_device, mesh=mesh, in_specs=placed, out_specs=P("kv", "ctx"), check_vma=False
    )
```

time: 313 us -> 157 us (0.50)
  the two profiles are of different devices: /device:TPU:25 before, /device:TPU:7 now
where the time goes in v2:
time: 157 us; the launch traced here: 156 us
  Pallas kernels  152 us (97%)
  local copies, waits for them, and re-layouts  3.02 us (2%)
    pallas_call x1, Pallas kernels, layer(): pl.pallas_call(body, in_specs=[smem] * 2 + [vmem] * 3 + [pl.BlockSpec(mem...  152 us

profile of v2, /device:TPU:7, one launch (start us, length us, event | category | flops | bytes accessed | tf_op | source)
XLA Modules:
  0.0 156.3 jit_solution(11856514252374309159)
XLA Ops:
  0.0 0.0 copy-start
  0.0 0.7 copy-done
  0.8 0.1 convert_reduce_fusion
  0.9 0.1 copy.24
  1.0 0.4 select_reduce_fusion
  1.4 0.1 copy.20
  1.5 0.0 copy-start.1
  1.5 0.1 fusion
  1.6 0.1 copy.22
  1.7 0.1 copy.23
  1.8 0.7 select_select_fusion.refs_1_
  2.5 0.0 copy-done.1
  2.5 152.0 %layer.1 = bf16[256,1024]{1,0:T(8,128)(2,1)} custom-call(s32[8,2,7]{2,1,0:T(2,128)} %copy-done.1, f32[8,2,7]{2,1,0:T(2,128)} %select_select_fusion.refs_1_, bf16[128,2048]{1,0:T(8,128)(2,1)} %refs_2_.1, bf16[32,128,256]{2,1,0:T(8,128)(2,1)} %bitcast.3, bf16[32,128,256]{2,1,0:T(8,128)(2,1)} %bitcast.4, bf16[2048,1024]{1,0:T(8,128)(2,1)} %refs_5_.1), custom_call_target="tpu_custom_call" | custom-call | tf_op jit(solution)/shard_map/layer/pallas_call | solution.py:394
  154.5 1.9 %copy.29 = bf16[256,1024]{1,0:T(8,128)(2,1)} copy(bf16[256,1024]{1,0:T(8,128)(2,1)} %layer.1) | data formatting | bytes 1048576
  (6 shorter events, 0.0 us)
Async XLA Ops:
  0.0 0.8 copy-start
  1.5 1.0 copy-start.1

commit v3 on v2

--- a/solution.py
+++ b/solution.py
@@ -252,26 +252,28 @@
             for copy in chip_copies(chip, at):
                 copy.start()
 
-    def each(step, visit):
-        def one(index, carry):
-            side, own_core = index % 2, index // 2
+    def two_sides(step, visit, between):
+        def one(turn, carry):
+            side = jnp.where(chip - step >= 0, turn, 1 - turn)
             at = jnp.where(side == 0, chip - step, chip + step)
-            valid = (at >= 0) & (at < chips) & ((step > 0) | (side == 0))
-
-            @pl.when(valid)
-            def _():
-                visit(at, own_core)
+
+            @pl.when((at >= 0) & (at < chips) & ((step > 0) | (turn == 0)))
+            def _():
+                visit(at)
+
+            @pl.when(turn == 0)
+            def _():
+                between(step + 1)
 
             return carry
 
-        return one
+        lax.fori_loop(0, 2, one, 0)
 
     q_all[me] = q_ref[...]
-
-    def attend_step(step, carry):
-        spread(q_all, q_send, q_recv, step)
-
-        def visit(at, own_core):
+    spread(q_all, q_send, q_recv, 0)
+
+    def attend_chip(at):
+        def one(own_core, carry):
             slot = at * 2 + jnp.where(own_core == 1, core, 1 - core)
 
             @pl.when(own_core == 0)
@@ -285,8 +287,13 @@
                 for copy in pair_copies(at):
                     copy.start()
 
-        lax.fori_loop(0, 4, each(step, visit), 0)
-        lax.fori_loop(0, 2, each(step, lambda at, own_core: merge_pair(at)), 0)
+            return carry
+
+        lax.fori_loop(0, 2, one, 0)
+        merge_pair(at)
+
+    def attend_step(step, carry):
+        two_sides(step, attend_chip, lambda later: spread(q_all, q_send, q_recv, later))
         return carry
 
     lax.fori_loop(0, chips, attend_step, 0)
@@ -315,25 +322,25 @@
 
     weight_copy.wait()
 
+    spread(merged_all, m_send, m_recv, 0)
+
+    def project_chip(at):
+        along(merged_all, m_send, m_recv, at * 2 + 1 - core, 2).wait_recv()
+        both = pl.ds(at * 2, 2)
+        product = jnp.dot(
+            merged_all[both].reshape(2 * tokens, columns),
+            weight[...],
+            preferred_element_type=jnp.float32,
+        )
+        projected[both] = product.astype(jnp.bfloat16).reshape(2, tokens, -1)
+
+        @pl.when(at * 2 // per_group != group_me)
+        def _():
+            for i in range(2):
+                group_copy(at * 2 + i, group_me).start()
+
     def project_step(step, carry):
-        spread(merged_all, m_send, m_recv, step)
-
-        def visit(at, own_core):
-            slot = at * 2 + jnp.where(own_core == 1, 1 - core, core)
-
-            @pl.when(own_core == 1)
-            def _():
-                along(merged_all, m_send, m_recv, slot, 2).wait_recv()
-
-            projected[slot] = jnp.dot(
-                merged_all[slot], weight[...], preferred_element_type=jnp.float32
-            ).astype(jnp.bfloat16)
-
-            @pl.when(slot // per_group != group_me)
-            def _():
-                group_copy(slot, group_me).start()
-
-        lax.fori_loop(0, 4, each(step, visit), 0)
+        two_sides(step, project_chip, lambda later: spread(merged_all, m_send, m_recv, later))
         return carry
 
     lax.fori_loop(0, chips, project_step, 0)

time: 157 us -> 153 us (0.975)
  the two profiles are of different devices: /device:TPU:7 before, /device:TPU:25 now
where the time goes in v3:
time: 153 us
  Pallas kernels  148 us (97%)
  local copies, waits for them, and re-layouts  3.02 us (2%)
    pallas_call x1, Pallas kernels, layer(): pl.pallas_call(body, in_specs=[smem] * 2 + [vmem] * 3 + [pl.BlockSpec(mem...  148 us

profile of v3, /device:TPU:25, one launch (start us, length us, event | category | flops | bytes accessed | tf_op | source)
XLA Modules:
  0.0 152.6 jit_solution(13083196851342112877)
XLA Ops:
  0.0 0.0 copy-start
  0.0 0.7 copy-done
  0.8 0.1 convert_reduce_fusion
  0.9 0.1 copy.24
  1.0 0.4 select_reduce_fusion
  1.4 0.1 copy.20
  1.5 0.0 copy-start.1
  1.5 0.1 fusion
  1.6 0.1 copy.22
  1.7 0.1 copy.23
  1.8 0.7 select_select_fusion.refs_1_
  2.5 0.0 copy-done.1
  2.5 148.2 %layer.1 = bf16[256,1024]{1,0:T(8,128)(2,1)} custom-call(s32[8,2,7]{2,1,0:T(2,128)} %copy-done.1, f32[8,2,7]{2,1,0:T(2,128)} %select_select_fusion.refs_1_, bf16[128,2048]{1,0:T(8,128)(2,1)} %refs_2_.1, bf16[32,128,256]{2,1,0:T(8,128)(2,1)} %bitcast.3, bf16[32,128,256]{2,1,0:T(8,128)(2,1)} %bitcast.4, bf16[2048,1024]{1,0:T(8,128)(2,1)} %refs_5_.1), custom_call_target="tpu_custom_call" | custom-call | tf_op jit(solution)/shard_map/layer/pallas_call | solution.py:401
  150.7 1.9 %copy.29 = bf16[256,1024]{1,0:T(8,128)(2,1)} copy(bf16[256,1024]{1,0:T(8,128)(2,1)} %layer.1) | data formatting | bytes 1048576
  (6 shorter events, 0.0 us)
Async XLA Ops:
  0.0 0.8 copy-start
  1.5 1.0 copy-start.1

commit v4 on v3

--- a/solution.py
+++ b/solution.py
@@ -37,6 +37,7 @@
     weight,
     projected,
     group_in,
+    corner_in,
     q_send,
     q_recv,
     m_send,
@@ -51,6 +52,7 @@
     chip_lse_recv,
     group_send,
     group_recv,
+    corner_recv,
     w_sem,
 ):
     me, group_me = lax.axis_index("ctx"), lax.axis_index("kv")
@@ -174,15 +176,65 @@
             ),
         )
 
-    def group_copy(slot, source):
-        inside = slot % per_group
+    beside = group_me + 1 - 2 * (group_me % 2)
+    across = (group_me + 2) % 4
+    corner = 3 - group_me
+
+    def group_copy(slot):
+        owner, inside = slot // per_group, slot % per_group
+        source = jnp.where(owner == beside, 0, 1)
         return remote(
             projected.at[slot],
             group_in.at[source, inside],
             group_send.at[slot],
             group_recv.at[source, inside],
-            {"kv": slot // per_group},
-        )
+            {"kv": owner},
+        )
+
+    def corner_copy(at, half):
+        return remote(
+            projected.at[at * 2 + half],
+            corner_in.at[at],
+            group_send.at[at * 2 + half],
+            corner_recv.at[at],
+            {"kv": across if half else beside},
+        )
+
+    def send_projected(at):
+        owner = at * 2 // per_group
+
+        @pl.when(owner == corner)
+        def _():
+            corner_copy(at, 0).start()
+            corner_copy(at, 1).start()
+
+        @pl.when(owner == beside)
+        def _():
+            group_copy(at * 2).start()
+
+        @pl.when(owner == across)
+        def _():
+            group_copy(at * 2 + 1).start()
+
+    def send_joined(at):
+        owner = at * 2 // per_group
+
+        @pl.when((owner == beside) | (owner == across))
+        def _():
+            corner_copy(at, 0).wait_recv()
+            slot = at * 2 + jnp.where(owner == beside, 1, 0)
+            joined = projected[slot].astype(jnp.float32) + corner_in[at].astype(jnp.float32)
+            projected[slot] = joined.astype(jnp.bfloat16)
+            group_copy(slot).start()
+
+    def join_step(step):
+        @pl.when((step >= 0) & (chip - step >= 0))
+        def _():
+            send_joined(chip - step)
+
+        @pl.when((step > 0) & (chip + step < chips))
+        def _():
+            send_joined(chip + step)
 
     def attend(slot):
         first = slot * tokens
@@ -334,22 +386,23 @@
         )
         projected[both] = product.astype(jnp.bfloat16).reshape(2, tokens, -1)
 
-        @pl.when(at * 2 // per_group != group_me)
-        def _():
-            for i in range(2):
-                group_copy(at * 2 + i, group_me).start()
+        send_projected(at)
 
     def project_step(step, carry):
         two_sides(step, project_chip, lambda later: spread(merged_all, m_send, m_recv, later))
+        join_step(step - 1)
         return carry
 
     lax.fori_loop(0, chips, project_step, 0)
+    join_step(chips - 1)
 
     def gather_groups(inside, carry):
         total = projected[group_me * per_group + inside].astype(jnp.float32)
-        for step in range(1, groups):
-            source = lax.rem(group_me + step, groups)
-            group_copy(group_me * per_group + inside, source).wait_recv()
+        for source in range(2):
+            arrived = group_in.at[source, inside]
+            remote(
+                arrived, arrived, group_send.at[0], group_recv.at[source, inside], {"kv": beside}
+            ).wait_recv()
             total += group_in[source, inside].astype(jnp.float32)
         out_ref[pl.ds(pl.multiple_of(inside * tokens, tokens), tokens), :] = total.astype(
             out_ref.dtype
@@ -377,7 +430,7 @@
     def finish_groups(slot, carry):
         @pl.when(slot // per_group != group_me)
         def _():
-            group_copy(slot, group_me).wait_send()
+            group_copy(slot).wait_send()
 
         return carry
 
@@ -416,7 +469,8 @@
             pltpu.VMEM((shards, tokens, columns), half),
             pltpu.VMEM(out_weight.shape, half),
             pltpu.VMEM((shards, tokens, wide), half),
-            pltpu.VMEM((groups, per_group, tokens, wide), half),
+            pltpu.VMEM((2, per_group, tokens, wide), half),
+            pltpu.VMEM((chips, tokens, wide), half),
             dma((3, shards)),
             dma((shards,)),
             dma((3, shards)),
@@ -430,7 +484,8 @@
             dma((chips,)),
             dma((chips,)),
             dma((shards,)),
-            dma((groups, per_group)),
+            dma((2, per_group)),
+            dma((chips,)),
             dma,
         ],
         compiler_params=pltpu.CompilerParams(

time: 153 us -> 146 us (0.954)
  Pallas kernels: 148 us -> 140 us
    pallas_call x1, Pallas kernels: 148 us -> 140 us  [layer(): pl.pallas_call(body, in_specs=[smem] * 2 + [vmem] * 3 + [pl.BlockSpec(mem...]
where the time goes in v4:
time: 146 us; the launch traced here: 144 us
  Pallas kernels  140 us (96%)
  local copies, waits for them, and re-layouts  3.02 us (2%)
    pallas_call x1, Pallas kernels, layer(): pl.pallas_call(body, in_specs=[smem] * 2 + [vmem] * 3 + [pl.BlockSpec(mem...  140 us

profile of v4, /device:TPU:25, one launch (start us, length us, event | category | flops | bytes accessed | tf_op | source)
XLA Modules:
  0.0 144.3 jit_solution(17967731738681945747)
XLA Ops:
  0.0 0.0 copy-start
  0.0 0.7 copy-done
  0.8 0.1 convert_reduce_fusion
  0.9 0.1 copy.24
  1.0 0.4 select_reduce_fusion
  1.4 0.1 copy.20
  1.5 0.0 copy-start.1
  1.5 0.1 fusion
  1.6 0.1 copy.22
  1.7 0.1 copy.23
  1.8 0.7 select_select_fusion.refs_1_
  2.5 0.0 copy-done.1
  2.5 139.9 %layer.1 = bf16[256,1024]{1,0:T(8,128)(2,1)} custom-call(s32[8,2,7]{2,1,0:T(2,128)} %copy-done.1, f32[8,2,7]{2,1,0:T(2,128)} %select_select_fusion.refs_1_, bf16[128,2048]{1,0:T(8,128)(2,1)} %refs_2_.1, bf16[32,128,256]{2,1,0:T(8,128)(2,1)} %bitcast.3, bf16[32,128,256]{2,1,0:T(8,128)(2,1)} %bitcast.4, bf16[2048,1024]{1,0:T(8,128)(2,1)} %refs_5_.1), custom_call_target="tpu_custom_call" | custom-call | tf_op jit(solution)/shard_map/layer/pallas_call | solution.py:454
  142.4 1.9 %copy.29 = bf16[256,1024]{1,0:T(8,128)(2,1)} copy(bf16[256,1024]{1,0:T(8,128)(2,1)} %layer.1) | data formatting | bytes 1048576
  (6 shorter events, 0.0 us)
Async XLA Ops:
  0.0 0.8 copy-start
  1.5 1.0 copy-start.1

commit v5 on v4

--- a/solution.py
+++ b/solution.py
@@ -239,7 +239,7 @@
     def attend(slot):
         first = slot * tokens
         block_index, offset = first // BLK, first % BLK
-        stack = max(1, min(per_list, 2 * BLK // tokens))
+        stack = max(1, min(per_list, 4 * BLK // tokens))
         rows = lax.broadcasted_iota(jnp.int32, (stack * tokens, BLK), 0) % tokens + offset
         places = lax.broadcasted_iota(jnp.int32, (stack * tokens, BLK), 1)
         lanes = lax.broadcasted_iota(jnp.int32, (tokens, BLK), 1)

time: 146 us -> 144 us (0.986)
  Pallas kernels: 140 us -> 137 us
    pallas_call x1, Pallas kernels: 140 us -> 137 us  [layer(): pl.pallas_call(body, in_specs=[smem] * 2 + [vmem] * 3 + [pl.BlockSpec(mem...]
where the time goes in v5:
time: 144 us; the launch traced here: 142 us
  Pallas kernels  137 us (95%)
  local copies, waits for them, and re-layouts  3.02 us (2%)
    pallas_call x1, Pallas kernels, layer(): pl.pallas_call(body, in_specs=[smem] * 2 + [vmem] * 3 + [pl.BlockSpec(mem...  137 us

profile of v5, /device:TPU:25, one launch (start us, length us, event | category | flops | bytes accessed | tf_op | source)
XLA Modules:
  0.0 141.6 jit_solution(11852099700283931343)
XLA Ops:
  0.0 0.0 copy-start
  0.0 0.7 copy-done
  0.8 0.1 convert_reduce_fusion
  0.9 0.1 copy.24
  1.0 0.4 select_reduce_fusion
  1.4 0.1 copy.20
  1.5 0.0 copy-start.1
  1.5 0.1 fusion
  1.6 0.1 copy.22
  1.7 0.1 copy.23
  1.8 0.7 select_select_fusion.refs_1_
  2.5 0.0 copy-done.1
  2.5 137.2 %layer.1 = bf16[256,1024]{1,0:T(8,128)(2,1)} custom-call(s32[8,2,7]{2,1,0:T(2,128)} %copy-done.1, f32[8,2,7]{2,1,0:T(2,128)} %select_select_fusion.refs_1_, bf16[128,2048]{1,0:T(8,128)(2,1)} %refs_2_.1, bf16[32,128,256]{2,1,0:T(8,128)(2,1)} %bitcast.3, bf16[32,128,256]{2,1,0:T(8,128)(2,1)} %bitcast.4, bf16[2048,1024]{1,0:T(8,128)(2,1)} %refs_5_.1), custom_call_target="tpu_custom_call" | custom-call | tf_op jit(solution)/shard_map/layer/pallas_call | solution.py:454
  139.7 1.9 %copy.29 = bf16[256,1024]{1,0:T(8,128)(2,1)} copy(bf16[256,1024]{1,0:T(8,128)(2,1)} %layer.1) | data formatting | bytes 1048576
  (6 shorter events, 0.0 us)
Async XLA Ops:
  0.0 0.8 copy-start
  1.5 1.0 copy-start.1
